TPU v7x, 512 devices: a whole 4x8x8 slice. The times are simulated.
512 devices in a mesh: dp: 512 (over y, z, x, core).
Axes of the slice: x: 4, y: 8, z: 8, core: 2. Of those that a mesh axis runs over, the one named last changes fastest.
Arguments:
- video_emb: bfloat16 [196608, 640], P('dp'), may hold values from -6 to 6
- captions: bfloat16 [196608, 1152], P('dp'), may hold values from -0.29882812 to 0.29882812
- projection: bfloat16 [1152, 640], replicated, may hold values from -0.0068359375 to 0.0068359375
- labels: int32 [196608], P('dp'), may hold values 0 or 1
- log_scale: float32 [1], replicated, may hold values from 1.5 to 2.5
- bias: float32 [1], replicated, may hold values from -3 to -1
Outputs:
- caption_grad: bfloat16 [196608, 1152], P('dp')
- projection_grad: bfloat16 [1152, 640], replicated
All inputs are finite; a program needn't handle non-finite values. No bound on the sum of `labels` on one device may be relied on, other than what follows from the above.
Results may differ from a plain program's by a relative error of at most 0.014.
Values may be sent and summed in bfloat16 or wider, within the bound.
A program may use at most 64 MiB of HBM per device.

v0:
```python
import jax
import jax.numpy as jnp
from jax import lax
from jax.sharding import PartitionSpec as P

ROUNDS = 4


def swapped(x, axis, apart):
    return lax.ppermute(x, axis, [(i, i ^ 1 << apart) for i in range(lax.axis_size(axis))])


def unit_rows(values):
    inverse = lax.rsqrt(jnp.sum(values * values, axis=-1, keepdims=True) + 1e-06)
    return (values * inverse, inverse)


def pair_terms(zvid, zcap, sign, scale, shift):
    logits = (
        scale
        * lax.dot_general(zvid, zcap, (((1,), (1,)), ((), ())), preferred_element_type=jnp.float32)
        + shift
    )
    if sign is None:
        weight = jax.nn.sigmoid(logits)
    else:
        weight = -sign * jax.nn.sigmoid(-sign * logits)
    weight = weight.astype(jnp.bfloat16)
    return scale * lax.dot_general(
        weight, zvid, (((0,), (0,)), ((), ())), preferred_element_type=jnp.float32
    )


def fetch_captions(zcap, bit):
    return swapped(zcap, "dp", bit)


def return_terms(terms, bit):
    return swapped(terms.astype(jnp.bfloat16), "dp", bit).astype(terms.dtype)


def local(video_emb, captions, projection, labels, log_scale, bias):
    rows = captions.shape[0]
    scale = jnp.exp(log_scale[0])
    shift = bias[0]
    zv = unit_rows(video_emb.astype(jnp.float32))[0].astype(jnp.bfloat16)
    hidden = jnp.dot(captions, projection, preferred_element_type=jnp.float32)
    zf, inverse = unit_rows(hidden)
    zc = zf.astype(jnp.bfloat16)
    positive = (labels == 1)[None, :] & jnp.eye(rows, dtype=bool)
    own_sign = jnp.where(positive, 1.0, -1.0).astype(jnp.float32)
    dz = pair_terms(zv, zc, own_sign, scale, shift)
    level = lax.axis_size("dp").bit_length() - 1
    bits = [step * (level - 1) // 3 for step in range(ROUNDS)]
    for bit in bits:
        visitor = fetch_captions(zc, bit)
        dz = dz + return_terms(pair_terms(zv, visitor, None, scale, shift), bit)
    dh = (inverse * (dz - zf * jnp.sum(zf * dz, axis=-1, keepdims=True))).astype(jnp.bfloat16)
    caption_grad = lax.dot_general(
        dh, projection, (((1,), (1,)), ((), ())), preferred_element_type=jnp.float32
    ).astype(jnp.bfloat16)
    term = lax.dot_general(
        captions, dh, (((0,), (0,)), ((), ())), preferred_element_type=jnp.float32
    )
    devices = lax.axis_size("dp")
    total = lax.psum(term, "dp")
    projection_grad = (total / devices).astype(jnp.bfloat16)
    return (caption_grad, projection_grad)


def solution(mesh):
    return jax.shard_map(
        local,
        mesh=mesh,
        in_specs=(P("dp", None), P("dp", None), P(), P("dp"), P(), P()),
        out_specs=(P("dp", None), P()),
        check_vma=False,
    )
```

profile of v0, /device:TPU:1, one launch (start us, length us, event | category | flops | bytes accessed | tf_op | source)
XLA Modules:
  0.0 391.5 jit_solution(17046231777114899164)
XLA Ops:
  7.2 0.0 copy-start
  7.2 0.0 all-reduce.2.cloned.1.call-start
  7.2 1.3 copy-done
  8.5 2.2 multiply_reduce_fusion.1
  10.7 0.0 copy-start.2
  10.7 0.9 multiply_convert_fusion.2
  11.6 8.8 %collective-permute-start = (bf16[384,640]{1,0:T(8,128)(2,1)}, bf16[384,640]{1,0:T(8,128)(2,1)S(1)}, u32[]{:S(2)}, u32[]{:S(2)}) collective-permute-start(bf16[384,640]{1,0:T(8,128)(2,1)} %multiply_convert_fusion.2), channel_id=1, source_target_pairs={{0,1},{1,0},{2,3},{3,2},{4,5},{5,4},{6,7},{7,6},{8,9},{9,8},{10,11... | collective-permute-start | bytes 1474568 | tf_op jit(solution)/shard_map/ppermute | solution.py:10
  20.4 1.9 collective-permute-start.2
  22.3 8.0 %collective-permute-start.4 = (bf16[384,640]{1,0:T(8,128)(2,1)}, bf16[384,640]{1,0:T(8,128)(2,1)}, u32[]{:S(2)}, u32[]{:S(2)}) collective-permute-start(bf16[384,640]{1,0:T(8,128)(2,1)} %multiply_convert_fusion.2), channel_id=1, source_target_pairs={{0,32},{1,33},{2,34},{3,35},{4,36},{5,37},{6,38},{7,39},{8,40},{9,... | collective-permute-start | bytes 1474568 | tf_op jit(solution)/shard_map/ppermute | solution.py:10
  30.4 7.5 %collective-permute-start.6 = (bf16[384,640]{1,0:T(8,128)(2,1)}, bf16[384,640]{1,0:T(8,128)(2,1)}, u32[]{:S(2)}, u32[]{:S(2)}) collective-permute-start(bf16[384,640]{1,0:T(8,128)(2,1)} %multiply_convert_fusion.2), channel_id=1, source_target_pairs={{0,256},{1,257},{2,258},{3,259},{4,260},{5,261},{6,262},{7,263},{8... | collective-permute-start | bytes 1474568 | tf_op jit(solution)/shard_map/ppermute | solution.py:10
  39.1 0.0 copy-done.2
  39.2 0.2 fusion.36
  39.3 0.0 collective-permute-done
  39.4 1.9 fusion
  41.2 2.7 collective-permute-start.1
  44.0 0.0 collective-permute-done.2
  44.0 2.9 fusion.1
  46.9 2.1 collective-permute-start.3
  49.0 0.0 collective-permute-done.4
  49.0 2.9 fusion.2
  51.9 1.9 collective-permute-start.5
  53.8 0.0 collective-permute-done.6
  53.8 0.0 copy-start.3
  53.8 2.9 fusion.3
  56.7 6.3 %collective-permute-start.7 = (bf16[384,640]{1,0:T(8,128)(2,1)}, bf16[384,640]{1,0:T(8,128)(2,1)}, u32[]{:S(2)}, u32[]{:S(2)}) collective-permute-start(bf16[384,640]{1,0:T(8,128)(2,1)} %fusion.3), channel_id=1, source_target_pairs={{0,256},{1,257},{2,258},{3,259},{4,260},{5,261},{6,262},{7,263},{8... | collective-permute-start | bytes 1474568 | tf_op jit(solution)/shard_map/ppermute | solution.py:10
  63.0 0.0 copy-done.3
  63.0 0.0 collective-permute-done.1
  63.1 0.4 collective-permute-done.3
  63.4 3.2 collective-permute-done.5
  66.6 4.2 %collective-permute-done.7 = bf16[384,640]{1,0:T(8,128)(2,1)} collective-permute-done((bf16[384,640]{1,0:T(8,128)(2,1)}, bf16[384,640]{1,0:T(8,128)(2,1)}, u32[]{:S(2)}, u32[]{:S(2)}) %collective-permute-start.7) | collective-permute-done | bytes 491552 | tf_op jit(solution)/shard_map/ppermute | solution.py:10
  70.8 3.6 multiply_reduce_fusion
  74.4 0.0 copy-start.1
  74.4 2.2 multiply_convert_fusion.1
  76.6 0.0 copy-done.1
  76.6 2.7 convolution_bitcast_fusion
  79.3 0.0 all-reduce.2.cloned.1.call-update
  79.3 1.8 convolution_convert_fusion
  81.1 299.4 %all-reduce.2.cloned.1.call-done = f32[1152,640]{0,1:T(8,128)} async-done(((f32[1152,640]{0,1:T(8,128)}), f32[1152,640]{0,1:T(8,128)}) %all-reduce.2.cloned.1.call-update) | async-done | bytes 2949136 | tf_op jit(solution)/shard_map/psum | solution.py:66
  380.6 2.0 multiply_convert_fusion
  382.6 2.1 copy.8
  (3 shorter events, 0.0 us)
Async XLA Ops:
  7.2 1.4 copy-start
  7.2 373.4 %all-reduce.2.cloned.1.call-start = ((), (), s32[]{:S(2)}) async-start(), calls=%async_computation | async-start | bytes 5898240 | tf_op jit(solution)/shard_map/psum | solution.py:66
  10.7 28.4 %copy-start.2 = (bf16[384,640]{1,0:T(8,128)(2,1)S(1)}, bf16[384,640]{1,0:T(8,128)(2,1)}, u32[]{:S(2)}) copy-start(bf16[384,640]{1,0:T(8,128)(2,1)} %param.6) | copy-start | bytes 1474564
  11.6 27.7 %collective-permute-start = (bf16[384,640]{1,0:T(8,128)(2,1)}, bf16[384,640]{1,0:T(8,128)(2,1)S(1)}, u32[]{:S(2)}, u32[]{:S(2)}) collective-permute-start(bf16[384,640]{1,0:T(8,128)(2,1)} %multiply_convert_fusion.2), channel_id=1, source_target_pairs={{0,1},{1,0},{2,3},{3,2},{4,5},{5,4},{6,7},{7,6},{8,9},{9,8},{10,11... | collective-permute-start | bytes 1474568 | tf_op jit(solution)/shard_map/ppermute | solution.py:10
  20.4 23.5 %collective-permute-start.2 = (bf16[384,640]{1,0:T(8,128)(2,1)}, bf16[384,640]{1,0:T(8,128)(2,1)}, u32[]{:S(2)}, u32[]{:S(2)}) collective-permute-start(bf16[384,640]{1,0:T(8,128)(2,1)} %multiply_convert_fusion.2), channel_id=1, source_target_pairs={{0,4},{1,5},{2,6},{3,7},{4,0},{5,1},{6,2},{7,3},{8,12},{9,13},{10,... | collective-permute-start | bytes 1474568 | tf_op jit(solution)/shard_map/ppermute | solution.py:10
  22.3 26.7 %collective-permute-start.4 = (bf16[384,640]{1,0:T(8,128)(2,1)}, bf16[384,640]{1,0:T(8,128)(2,1)}, u32[]{:S(2)}, u32[]{:S(2)}) collective-permute-start(bf16[384,640]{1,0:T(8,128)(2,1)} %multiply_convert_fusion.2), channel_id=1, source_target_pairs={{0,32},{1,33},{2,34},{3,35},{4,36},{5,37},{6,38},{7,39},{8,40},{9,... | collective-permute-start | bytes 1474568 | tf_op jit(solution)/shard_map/ppermute | solution.py:10
  30.4 23.5 %collective-permute-start.6 = (bf16[384,640]{1,0:T(8,128)(2,1)}, bf16[384,640]{1,0:T(8,128)(2,1)}, u32[]{:S(2)}, u32[]{:S(2)}) collective-permute-start(bf16[384,640]{1,0:T(8,128)(2,1)} %multiply_convert_fusion.2), channel_id=1, source_target_pairs={{0,256},{1,257},{2,258},{3,259},{4,260},{5,261},{6,262},{7,263},{8... | collective-permute-start | bytes 1474568 | tf_op jit(solution)/shard_map/ppermute | solution.py:10
  41.2 21.8 %collective-permute-start.1 = (bf16[384,640]{1,0:T(8,128)(2,1)}, bf16[384,640]{1,0:T(8,128)(2,1)S(1)}, u32[]{:S(2)}, u32[]{:S(2)}) collective-permute-start(bf16[384,640]{1,0:T(8,128)(2,1)} %fusion), channel_id=1, source_target_pairs={{0,1},{1,0},{2,3},{3,2},{4,5},{5,4},{6,7},{7,6},{8,9},{9,8},{10,11... | collective-permute-start | bytes 1474568 | tf_op jit(solution)/shard_map/ppermute | solution.py:10
  46.9 16.6 %collective-permute-start.3 = (bf16[384,640]{1,0:T(8,128)(2,1)}, bf16[384,640]{1,0:T(8,128)(2,1)}, u32[]{:S(2)}, u32[]{:S(2)}) collective-permute-start(bf16[384,640]{1,0:T(8,128)(2,1)} %fusion.1), channel_id=1, source_target_pairs={{0,4},{1,5},{2,6},{3,7},{4,0},{5,1},{6,2},{7,3},{8,12},{9,13},{10,... | collective-permute-start | bytes 1474568 | tf_op jit(solution)/shard_map/ppermute | solution.py:10
  51.9 14.7 %collective-permute-start.5 = (bf16[384,640]{1,0:T(8,128)(2,1)}, bf16[384,640]{1,0:T(8,128)(2,1)}, u32[]{:S(2)}, u32[]{:S(2)}) collective-permute-start(bf16[384,640]{1,0:T(8,128)(2,1)} %fusion.2), channel_id=1, source_target_pairs={{0,32},{1,33},{2,34},{3,35},{4,36},{5,37},{6,38},{7,39},{8,40},{9,... | collective-permute-start | bytes 1474568 | tf_op jit(solution)/shard_map/ppermute | solution.py:10
  53.8 9.2 %copy-start.3 = (s32[384]{0:T(512)S(1)}, s32[384]{0:T(512)}, u32[]{:S(2)}) copy-start(s32[384]{0:T(512)} %param.9) | copy-start | bytes 4612
  56.7 14.1 %collective-permute-start.7 = (bf16[384,640]{1,0:T(8,128)(2,1)}, bf16[384,640]{1,0:T(8,128)(2,1)}, u32[]{:S(2)}, u32[]{:S(2)}) collective-permute-start(bf16[384,640]{1,0:T(8,128)(2,1)} %fusion.3), channel_id=1, source_target_pairs={{0,256},{1,257},{2,258},{3,259},{4,260},{5,261},{6,262},{7,263},{8... | collective-permute-start | bytes 1474568 | tf_op jit(solution)/shard_map/ppermute | solution.py:10
  74.4 2.2 copy-start.1
Sparse Core Ops, SparseCore 0:
  79.4 301.1 all-reduce.1
where the time goes:
time: 393 us; the launch traced here: 392 us
  waiting for transfers between devices  307 us (78%)
  starting transfers between devices  39.3 us (10%)
  matrix products  20.8 us (5%)
  between operations  15.5 us (4%)
  other arithmetic  5.28 us (1%)
    psum x1, waiting for transfers between devices, local(): total = lax.psum(term, 'dp')  299 us
    ppermute x8, starting transfers between devices, swapped(): lax.ppermute(x, axis, [(i, i ^ 1 << apart) for i in range(lax.axis_size(a...  39.2 us
    dot_general x5, matrix products, pair_terms(): lax.dot_general(weight, zvid, (((0,), (0,)), ((), ())), preferred_element...  14.2 us
  transfers between devices with their start and end apart: 9, of which 4 were waited for; matrix products, arithmetic and copies ran while one was open for 3% of the time, Pallas kernels for 0%

commit v1 on v0

v1 whole, which is shorter than its diff:
```python
import functools

import jax
import jax.numpy as jnp
from jax import lax
from jax.experimental import pallas as pl
from jax.experimental.pallas import tpu as pltpu
from jax.sharding import PartitionSpec as P

MESH = pl.DeviceIdType.MESH
F32 = jnp.float32
BF16 = jnp.bfloat16

AXES = {"core": (1, 2), "x": (2, 4), "z": (8, 8), "y": (64, 8)}
SIZE = {axis: size for axis, (_, size) in AXES.items()}

ROWS = 384
E = 640
D = 1152
HALF = D // 2
CHUNKS = 3
CHUNK = ROWS // (2 * CHUNKS)
LANES = 128
COLS = E // LANES

ORDERS = (("x", "y", "z"), ("y", "z", "x"), ("z", "x", "y"))
PARTS = len(ORDERS)
PART = HALF // PARTS
FLAT = PART * COLS
FULL = 1024


def place(me, axis):
    stride, size = AXES[axis]
    return lax.rem(lax.div(me, stride), size)


def shifted(me, axis, by):
    stride, size = AXES[axis]
    here = place(me, axis)
    return me + (lax.rem(here + (by + size), size) - here) * stride


def remote(src, dst, send, recv, device):
    return pltpu.make_async_remote_copy(
        src_ref=src, dst_ref=dst, send_sem=send, recv_sem=recv, device_id=(device,), device_id_type=MESH
    )


def far_first(size):
    return sorted(range(1, size), key=lambda by: -min(by, size - by))


def kernel(
    video_ref, captions_ref, projection_ref, labels_ref, log_scale_ref, bias_ref,
    cgrad_ref, pgrad_ref,
    video, captions, projection, flipped, zf, zc, inv, dz, dh, cgrad,
    own_core, own_x, relay_x, pool, relay,
    out_core, in_core, own_term,
    s1_out, s1_in, s2_out, s2_in, s3_in, gather2, gather1,
    load_sem, swap_send, swap_recv, hop_send, hop_recv, core_send, core_recv,
    stage_send, stage_recv, last_sem, last_send, last_recv,
):
    me = lax.axis_index("dp")
    core = place(me, "core")
    sibling = shifted(me, "core", 1)

    loads = [
        pltpu.make_async_copy(video_ref, video, load_sem.at[0]),
        pltpu.make_async_copy(captions_ref, captions, load_sem.at[1]),
        pltpu.make_async_copy(projection_ref, projection, load_sem.at[2]),
    ]
    for load in loads:
        load.start()

    barrier = pltpu.get_barrier_semaphore()
    greeted = 0
    for axis, size in SIZE.items():
        for by in range(1, size):
            pl.semaphore_signal(barrier, inc=1, device_id=(shifted(me, axis, by),), device_id_type=MESH)
            greeted += 1
    pl.semaphore_wait(barrier, greeted)
    loads[0].wait()

    ways = [("y", 1, 2), ("y", -1, 2), ("z", 1, 2), ("z", -1, 2), ("x", 1, 1), ("x", -1, 1)]
    hops = []
    for q in range(CHUNKS):
        for w, (axis, way, step) in enumerate(ways):
            rows = pl.ds(((0 if way > 0 else CHUNKS) + q) * CHUNK, CHUNK)
            if axis == "x":
                middle, final = relay_x.at[rows], own_x.at[rows]
            else:
                middle, final = relay.at[w, q], pool.at[q, pl.ds(w * CHUNK, CHUNK)]
            to = shifted(me, axis, way * step)
            first = remote(video.at[rows], middle, hop_send.at[w, q, 0], hop_recv.at[w, q, 0], to)
            second = remote(middle, final, hop_send.at[w, q, 1], hop_recv.at[w, q, 1], to)
            first.start()
            hops.append((first, second))
        if q == 0:
            swap = remote(video, own_core, swap_send, swap_recv, sibling)
            swap.start()

    def pass_on(q):
        for first, second in hops[q * len(ways):(q + 1) * len(ways)]:
            first.wait_recv()
            second.start()

    scale = jnp.exp(jnp.full((1, 1), log_scale_ref[0], F32))
    shift = bias_ref[0]

    loads[1].wait()
    loads[2].wait()
    hidden = jnp.dot(captions[...], projection[...], preferred_element_type=F32)
    inverse = lax.rsqrt(jnp.sum(hidden * hidden, axis=-1, keepdims=True) + 1e-06)
    unit = hidden * inverse
    zf[...] = unit
    zc[...] = unit.astype(BF16)
    inv[...] = inverse

    def pairing(rows, sign=None):
        raw = rows.astype(F32)
        zv = (raw * lax.rsqrt(jnp.sum(raw * raw, axis=-1, keepdims=True) + 1e-06)).astype(BF16)
        logits = scale * lax.dot_general(
            zc[...], zv, (((1,), (1,)), ((), ())), preferred_element_type=F32
        ) + shift
        if sign is None:
            weight = 1.0 / (1.0 + jnp.exp(-logits))
        else:
            weight = sign / (1.0 + jnp.exp(-sign * logits))
        return jnp.dot(weight.astype(BF16), zv, preferred_element_type=F32)

    pass_on(0)
    row = lax.broadcasted_iota(jnp.int32, (ROWS, ROWS), 0)
    column = lax.broadcasted_iota(jnp.int32, (ROWS, ROWS), 1)
    sign = jnp.where((row == column) & (labels_ref[...] == 1), -1.0, 1.0).astype(F32)
    dz[...] = pairing(video[...], sign)
    pass_on(1)
    swap.wait_recv()
    dz[...] += pairing(own_core[...])
    pass_on(2)
    flipped[...] = captions[...].T
    for q in range(CHUNKS):
        for first, second in hops[q * len(ways) + 4:(q + 1) * len(ways)]:
            second.wait_recv()
    dz[...] += pairing(own_x[...])
    for q in range(CHUNKS):
        for first, second in hops[q * len(ways):q * len(ways) + 4]:
            second.wait_recv()
        dz[...] += pairing(pool[q])

    total = scale * dz[...]
    along = jnp.sum(zf[...] * total, axis=-1, keepdims=True)
    dh[...] = (inv[...] * (total - zf[...] * along)).astype(BF16)

    def term(half, part):
        rows = pl.ds(pl.multiple_of(half * HALF + part * PART, 16), PART)
        return jnp.dot(flipped[rows, :], dh[...], preferred_element_type=F32)

    to_core = []
    for p in range(PARTS):
        value = term(1 - core, p).astype(BF16)
        for j in range(COLS):
            out_core[p, j * PART:(j + 1) * PART, :] = value[:, j * LANES:(j + 1) * LANES]
        copy = remote(out_core.at[p], in_core.at[p], core_send.at[p], core_recv.at[p], sibling)
        copy.start()
        to_core.append(copy)
    for p in range(PARTS):
        value = term(core, p)
        for j in range(COLS):
            own_term[p, j * PART:(j + 1) * PART, :] = value[:, j * LANES:(j + 1) * LANES]

    pending = list(to_core)

    def start_all(stage, p, axis, src_of, dst_of):
        copies = []
        for by in far_first(SIZE[axis]):
            copy = remote(
                src_of(by), dst_of(by), stage_send.at[stage, p, by], stage_recv.at[stage, p, by], shifted(me, axis, by)
            )
            copy.start()
            copies.append(copy)
        pending.extend(copies)
        return copies

    arrivals = [None] * PARTS
    for p, (axis, _, _) in enumerate(ORDERS):
        to_core[p].wait_recv()
        s1_out[p, :FLAT, :] = (own_term[p] + in_core[p].astype(F32)).astype(BF16)
        s1_out[p, FLAT:, :] = jnp.zeros((FULL - FLAT, LANES), BF16)
        n = SIZE[axis]
        rows = FULL // n
        here = place(me, axis)
        arrivals[p] = start_all(
            0, p, axis,
            lambda by: s1_out.at[p, pl.ds(pl.multiple_of(lax.rem(here + by, n) * rows, 16), rows)],
            lambda by: s1_in.at[p, by, pl.ds(0, rows)],
        )

    cgrad[...] = lax.dot_general(
        dh[...], projection[...], (((1,), (1,)), ((), ())), preferred_element_type=F32
    ).astype(BF16)
    store = pltpu.make_async_copy(cgrad, cgrad_ref, last_sem.at[0])
    store.start()

    for p, (axis1, axis2, _) in enumerate(ORDERS):
        for copy in arrivals[p]:
            copy.wait_recv()
        n1, n2 = SIZE[axis1], SIZE[axis2]
        rows1 = FULL // n1
        rows2 = rows1 // n2
        mine = pl.ds(pl.multiple_of(place(me, axis1) * rows1, 16), rows1)
        value = s1_out[p, mine, :].astype(F32)
        for by in range(1, n1):
            value += s1_in[p, by, :rows1, :].astype(F32)
        s2_out[p, :rows1, :] = value.astype(BF16)
        here = place(me, axis2)
        arrivals[p] = start_all(
            1, p, axis2,
            lambda by: s2_out.at[p, pl.ds(pl.multiple_of(lax.rem(here + by, n2) * rows2, 16), rows2)],
            lambda by: s2_in.at[p, by, pl.ds(0, rows2)],
        )

    for p, (axis1, axis2, axis3) in enumerate(ORDERS):
        for copy in arrivals[p]:
            copy.wait_recv()
        n2 = SIZE[axis2]
        rows2 = FULL // SIZE[axis1] // n2
        mine = pl.ds(pl.multiple_of(place(me, axis2) * rows2, 16), rows2)
        value = s2_out[p, mine, :].astype(F32)
        for by in range(1, n2):
            value += s2_in[p, by, :rows2, :].astype(F32)
        here = place(me, axis3)
        s3_in[p, here, :rows2, :] = value.astype(BF16)
        slot = s3_in.at[p, here, pl.ds(0, rows2)]
        arrivals[p] = start_all(2, p, axis3, lambda by: slot, lambda by: slot)

    devices = 1
    for size in SIZE.values():
        devices *= size

    for p, (axis1, axis2, axis3) in enumerate(ORDERS):
        for copy in arrivals[p]:
            copy.wait_recv()
        rows2 = FULL // SIZE[axis1] // SIZE[axis2]
        value = s3_in[p, 0, :rows2, :].astype(F32)
        for k in range(1, SIZE[axis3]):
            value += s3_in[p, k, :rows2, :].astype(F32)
        mine = pl.ds(pl.multiple_of(place(me, axis2) * rows2, 16), rows2)
        gather2[p, mine, :] = (value / devices).astype(BF16)
        slot = gather2.at[p, mine]
        arrivals[p] = start_all(3, p, axis2, lambda by: slot, lambda by: slot)

    for p, (axis1, _, _) in enumerate(ORDERS):
        for copy in arrivals[p]:
            copy.wait_recv()
        rows1 = FULL // SIZE[axis1]
        mine = pl.ds(pl.multiple_of(place(me, axis1) * rows1, 16), rows1)
        gather1[p, mine, :] = gather2[p, :rows1, :]
        slot = gather1.at[p, mine]
        arrivals[p] = start_all(4, p, axis1, lambda by: slot, lambda by: slot)

    writes = []
    for p in range(PARTS):
        for copy in arrivals[p]:
            copy.wait_recv()
        for j in range(COLS):
            src = gather1.at[p, pl.ds(j * PART, PART)]
            dst = pgrad_ref.at[
                pl.ds(pl.multiple_of(core * HALF + p * PART, 16), PART), pl.ds(j * LANES, LANES)
            ]
            copy = remote(src, dst, last_send.at[p, j], last_recv.at[p, j], sibling)
            copy.start()
            write = pltpu.make_async_copy(src, dst, last_sem.at[1 + p * COLS + j])
            write.start()
            writes.append((copy, write))
    for copy, write in writes:
        copy.wait()
        write.wait()

    store.wait()
    swap.wait_send()
    for first, second in hops:
        first.wait_send()
        second.wait_send()
    for copy in pending:
        copy.wait_send()


def local(video_emb, captions, projection, labels, log_scale, bias):
    dma = pltpu.SemaphoreType.DMA
    vmem = pltpu.VMEM
    shard = FULL // 4
    return pl.pallas_call(
        kernel,
        out_shape=(
            jax.ShapeDtypeStruct((ROWS, D), BF16),
            jax.ShapeDtypeStruct((D, E), BF16),
        ),
        in_specs=[pl.BlockSpec(memory_space=pl.ANY)] * 3
        + [pl.BlockSpec(memory_space=pltpu.VMEM)]
        + [pl.BlockSpec(memory_space=pltpu.SMEM)] * 2,
        out_specs=[pl.BlockSpec(memory_space=pl.ANY)] * 2,
        scratch_shapes=[
            vmem((ROWS, E), BF16),
            vmem((ROWS, D), BF16),
            vmem((D, E), BF16),
            vmem((D, ROWS), BF16),
            vmem((ROWS, E), F32),
            vmem((ROWS, E), BF16),
            vmem((ROWS, 1), F32),
            vmem((ROWS, E), F32),
            vmem((ROWS, E), BF16),
            vmem((ROWS, D), BF16),
            vmem((ROWS, E), BF16),
            vmem((ROWS, E), BF16),
            vmem((ROWS, E), BF16),
            vmem((CHUNKS, 4 * CHUNK, E), BF16),
            vmem((4, CHUNKS, CHUNK, E), BF16),
            vmem((PARTS, FLAT, LANES), BF16),
            vmem((PARTS, FLAT, LANES), BF16),
            vmem((PARTS, FLAT, LANES), F32),
            vmem((PARTS, FULL, LANES), BF16),
            vmem((PARTS, 8, shard, LANES), BF16),
            vmem((PARTS, shard, LANES), BF16),
            vmem((PARTS, 8, 32, LANES), BF16),
            vmem((PARTS, 8, 32, LANES), BF16),
            vmem((PARTS, shard, LANES), BF16),
            vmem((PARTS, FULL, LANES), BF16),
            dma((3,)),
            dma,
            dma,
            dma((6, CHUNKS, 2)),
            dma((6, CHUNKS, 2)),
            dma((PARTS,)),
            dma((PARTS,)),
            dma((5, PARTS, 8)),
            dma((5, PARTS, 8)),
            dma((1 + PARTS * COLS,)),
            dma((PARTS, COLS)),
            dma((PARTS, COLS)),
        ],
        compiler_params=pltpu.CompilerParams(
            collective_id=0, has_side_effects=True, vmem_limit_bytes=48 << 20
        ),
    )(video_emb, captions, projection, labels.reshape(1, -1), log_scale, bias)


def solution(mesh):
    return jax.shard_map(
        local,
        mesh=mesh,
        in_specs=(P("dp", None), P("dp", None), P(), P("dp"), P(), P()),
        out_specs=(P("dp", None), P()),
        check_vma=False,
    )
```

time: 393 us -> 84.4 us (0.21)
  waiting for transfers between devices: 307 us -> 0 us
  Pallas kernels: 0 us -> 75.9 us
  starting transfers between devices: 39.3 us -> 0 us
  matrix products: 20.8 us -> 0 us
  between operations: 15.5 us -> 1.93 us
  other arithmetic: 5.28 us -> 0 us
    psum x1 -> x0, waiting for transfers between devices: 299 us -> none  [local(): total = lax.psum(term, 'dp')]
    pallas_call x0 -> x1, Pallas kernels: none -> 75.9 us  [local(): pl.pallas_call(kernel, out_shape=(jax.ShapeDtypeStruct((ROWS, D), BF16),...]
    ppermute x8 -> x0, starting transfers between devices: 39.2 us -> none  [swapped(): lax.ppermute(x, axis, [(i, i ^ 1 << apart) for i in range(lax.axis_size(a...]
    dot_general x8 -> x0, matrix products: 20.8 us -> none  [the longest x5 14.2 us: pair_terms(): lax.dot_general(weight, zvid, (((0,), (0,)), ((), ())), preferred_element...]
    ppermute x8 -> x0, waiting for transfers between devices: 7.75 us -> none  [swapped(): lax.ppermute(x, axis, [(i, i ^ 1 << apart) for i in range(lax.axis_size(a...]
    convert_element_type x3 -> x0, other arithmetic: 5.09 us -> none  [the longest x1 2.15 us: local(): (inverse * (dz - zf * jnp.sum(zf * dz, axis=-1, keepdims=True))).astype(j...]
  transfers between devices with their start and end apart: 9 -> 0, of which waited for: 4 -> 0; matrix products, arithmetic and copies ran while one was open for 3% -> 0% of each run, Pallas kernels for 0% -> 0%
where the time goes in v1:
time: 84.4 us; the launch traced here: 84.1 us
  Pallas kernels  75.9 us (90%)
  local copies, waits for them, and re-layouts  6.28 us (7%)
  between operations  1.93 us (2%)
    pallas_call x1, Pallas kernels, local(): pl.pallas_call(kernel, out_shape=(jax.ShapeDtypeStruct((ROWS, D), BF16),...  75.9 us
    unnamed x8, local copies, waits for them, and re-layouts  5.59 us

profile of v1, /device:TPU:1, one launch (start us, length us, event | category | flops | bytes accessed | tf_op | source)
XLA Modules:
  0.0 84.1 jit_solution(10132897858574560111)
XLA Ops:
  1.9 0.7 reshape.7.labels_ref
  2.6 0.0 copy-start
  2.6 1.4 %copy-done = bf16[1152,640]{1,0:T(8,128)(2,1)S(1)} copy-done((bf16[1152,640]{1,0:T(8,128)(2,1)S(1)}, bf16[1152,640]{1,0:T(8,128)(2,1)}, u32[]{:S(2)}) %copy-start) | copy-done | bytes 1474584
  4.0 0.0 copy-start.1
  4.0 1.2 %copy-done.1 = bf16[384,1152]{1,0:T(8,128)(2,1)S(1)} copy-done((bf16[384,1152]{1,0:T(8,128)(2,1)S(1)}, bf16[384,1152]{1,0:T(8,128)(2,1)}, u32[]{:S(2)}) %copy-start.1) | copy-done | bytes 884760
  5.1 0.0 copy-start.2
  5.2 1.0 %copy-done.2 = bf16[384,640]{1,0:T(8,128)(2,1)S(1)} copy-done((bf16[384,640]{1,0:T(8,128)(2,1)S(1)}, bf16[384,640]{1,0:T(8,128)(2,1)}, u32[]{:S(2)}) %copy-start.2) | copy-done | bytes 491544
  6.2 75.9 %shard_map.77 = (bf16[384,1152]{1,0:T(8,128)(2,1)S(1)}, bf16[1152,640]{1,0:T(8,128)(2,1)S(1)}) custom-call(bf16[384,640]{1,0:T(8,128)(2,1)S(1)} %copy-done.2, bf16[384,1152]{1,0:T(8,128)(2,1)S(1)} %copy-done.1, bf16[1152,640]{1,0:T(8,128)(2,1)S(1)} %copy-done, s32[1,384]{1,0:T(1,128)S(1)} %reshape.7.labels_ref, f32[1]{0:T(128)S(6)} %copy.10.log_scale_ref, ...), custom_call_target="tpu_custom_call" | custom-call | tf_op jit(solution)/shard_map/pallas_call | solution.py:293
  82.1 0.9 %copy.12 = bf16[384,1152]{1,0:T(8,128)(2,1)} copy(bf16[384,1152]{1,0:T(8,128)(2,1)S(1)} %get-tuple-element.4) | data formatting | bytes 1769472
  83.0 1.1 %copy.13 = bf16[1152,640]{1,0:T(8,128)(2,1)} copy(bf16[1152,640]{1,0:T(8,128)(2,1)S(1)} %get-tuple-element.5) | data formatting | bytes 2949120
Async XLA Ops:
  2.6 1.4 %copy-start = (bf16[1152,640]{1,0:T(8,128)(2,1)S(1)}, bf16[1152,640]{1,0:T(8,128)(2,1)}, u32[]{:S(2)}) copy-start(bf16[1152,640]{1,0:T(8,128)(2,1)} %projection_ref.1) | copy-start | bytes 4423684
  4.0 1.2 %copy-start.1 = (bf16[384,1152]{1,0:T(8,128)(2,1)S(1)}, bf16[384,1152]{1,0:T(8,128)(2,1)}, u32[]{:S(2)}) copy-start(bf16[384,1152]{1,0:T(8,128)(2,1)} %captions_ref.1) | copy-start | bytes 2654212
  5.1 1.0 %copy-start.2 = (bf16[384,640]{1,0:T(8,128)(2,1)S(1)}, bf16[384,640]{1,0:T(8,128)(2,1)}, u32[]{:S(2)}) copy-start(bf16[384,640]{1,0:T(8,128)(2,1)} %video_ref.1) | copy-start | bytes 1474564

commit v2 on v1

v2 whole, which is shorter than its diff:
```python
import functools

import jax
import jax.numpy as jnp
from jax import lax
from jax.experimental import pallas as pl
from jax.experimental.pallas import tpu as pltpu
from jax.sharding import PartitionSpec as P

MESH = pl.DeviceIdType.MESH
F32 = jnp.float32
BF16 = jnp.bfloat16

AXES = {"core": (1, 2), "x": (2, 4), "z": (8, 8), "y": (64, 8)}
SIZE = {axis: size for axis, (_, size) in AXES.items()}

ROWS = 384
E = 640
D = 1152
HALF = D // 2
CHUNKS = 3
CHUNK = ROWS // CHUNKS
LANES = 128
COLS = E // LANES
TILE = 16

ORDERS = (("y", "z", "x"), ("z", "x", "y"), ("x", "y", "z"))
PART = (144, 144, 288)
FIRST = (0, 144, 288)
PARTS = len(ORDERS)


def up(value, multiple):
    return -(-value // multiple) * multiple


FLAT = tuple(rows * COLS for rows in PART)
SUM1 = tuple(up(-(-FLAT[p] // SIZE[ORDERS[p][0]]), TILE) for p in range(PARTS))
SUM2 = tuple(up(-(-SUM1[p] // SIZE[ORDERS[p][1]]), TILE) for p in range(PARTS))
FULL1 = tuple(SUM1[p] * SIZE[ORDERS[p][0]] for p in range(PARTS))
FULL2 = tuple(SUM2[p] * SIZE[ORDERS[p][1]] for p in range(PARTS))


def place(me, axis):
    stride, size = AXES[axis]
    return lax.rem(lax.div(me, stride), size)


def shifted(me, axis, by):
    stride, size = AXES[axis]
    here = place(me, axis)
    return me + (lax.rem(here + (by + size), size) - here) * stride


def remote(src, dst, send, recv, device):
    return pltpu.make_async_remote_copy(
        src_ref=src, dst_ref=dst, send_sem=send, recv_sem=recv, device_id=(device,), device_id_type=MESH
    )


def far_first(size):
    return sorted(range(1, size), key=lambda by: -min(by, size - by))


def kernel(
    video_ref, captions_ref, projection_ref, labels_ref, log_scale_ref, bias_ref,
    cgrad_ref, pgrad_ref,
    video, captions, projection, flipped, zf, zc, inv, dz, dh, cgrad,
    own_core, own_x, pool,
    out_core, in_core, own_term, s1_out, s1_in, s2_out, s2_in, s3_in, gather2, gather1, result,
    load_sem, swap_send, swap_recv, core_send, core_recv,
    stage_send, stage_recv, last_sem, last_send, last_recv, round_sem,
):
    me = lax.axis_index("dp")
    core = place(me, "core")
    sibling = shifted(me, "core", 1)

    loads = [
        pltpu.make_async_copy(video_ref, video, load_sem.at[0]),
        pltpu.make_async_copy(captions_ref, captions, load_sem.at[1]),
        pltpu.make_async_copy(projection_ref, projection, load_sem.at[2]),
    ]
    for load in loads:
        load.start()

    barrier = pltpu.get_barrier_semaphore()
    greeted = [(axis, SIZE[axis] // 2) for axis in ("y", "z", "x")]
    greeted += [(axis, by) for axis in ("y", "z", "x") for by in (1, -1)] + [("core", 1)]
    for axis, by in greeted:
        pl.semaphore_signal(barrier, inc=1, device_id=(shifted(me, axis, by),), device_id_type=MESH)
    pl.semaphore_wait(barrier, len(greeted))
    loads[0].wait()

    swaps = []
    for q in range(CHUNKS):
        rows = pl.ds(q * CHUNK, CHUNK)
        for w, axis in enumerate(("y", "z")):
            swap = remote(
                video.at[rows], pool.at[q, pl.ds(w * CHUNK, CHUNK)], swap_send.at[w, q], swap_recv.at[w, q],
                shifted(me, axis, SIZE[axis] // 2),
            )
            swap.start()
            swaps.append(swap)
        if q == 0:
            swap_x = remote(video, own_x, swap_send.at[2, 0], swap_recv.at[2, 0], shifted(me, "x", SIZE["x"] // 2))
            swap_x.start()
            swap_core = remote(video, own_core, swap_send.at[3, 0], swap_recv.at[3, 0], sibling)
            swap_core.start()

    neighbours = [("y", 1), ("y", -1), ("z", 1), ("z", -1)]
    for axis, by in neighbours:
        pl.semaphore_signal(round_sem, inc=1, device_id=(shifted(me, axis, by),), device_id_type=MESH)

    scale = jnp.exp(jnp.full((1, 1), log_scale_ref[0], F32))
    shift = bias_ref[0]

    loads[1].wait()
    loads[2].wait()
    hidden = jnp.dot(captions[...], projection[...], preferred_element_type=F32)
    inverse = lax.rsqrt(jnp.sum(hidden * hidden, axis=-1, keepdims=True) + 1e-06)
    unit = hidden * inverse
    zf[...] = unit
    zc[...] = unit.astype(BF16)
    inv[...] = inverse

    def pairing(rows, sign=None):
        raw = rows.astype(F32)
        zv = (raw * lax.rsqrt(jnp.sum(raw * raw, axis=-1, keepdims=True) + 1e-06)).astype(BF16)
        logits = scale * lax.dot_general(
            zc[...], zv, (((1,), (1,)), ((), ())), preferred_element_type=F32
        ) + shift
        if sign is None:
            weight = 1.0 / (1.0 + jnp.exp(-logits))
        else:
            weight = sign / (1.0 + jnp.exp(-sign * logits))
        return jnp.dot(weight.astype(BF16), zv, preferred_element_type=F32)

    row = lax.broadcasted_iota(jnp.int32, (ROWS, ROWS), 0)
    column = lax.broadcasted_iota(jnp.int32, (ROWS, ROWS), 1)
    sign = jnp.where((row == column) & (labels_ref[...].reshape(1, ROWS) == 1), -1.0, 1.0).astype(F32)
    dz[...] = pairing(video[...], sign)
    flipped[...] = captions[...].T
    pl.semaphore_wait(round_sem, len(neighbours))
    swap_core.wait_recv()
    dz[...] += pairing(own_core[...])
    swap_x.wait_recv()
    dz[...] += pairing(own_x[...])
    for q in range(CHUNKS):
        for swap in swaps[2 * q:2 * q + 2]:
            swap.wait_recv()
        dz[...] += pairing(pool[q])

    total = scale * dz[...]
    along = jnp.sum(zf[...] * total, axis=-1, keepdims=True)
    dh[...] = (inv[...] * (total - zf[...] * along)).astype(BF16)

    def term(half, part):
        rows = pl.ds(pl.multiple_of(half * HALF + FIRST[part], TILE), PART[part])
        return jnp.dot(flipped[rows, :], dh[...], preferred_element_type=F32)

    to_core = []
    for p in range(PARTS):
        value = term(1 - core, p).astype(BF16)
        for j in range(COLS):
            out_core[p][j * PART[p]:(j + 1) * PART[p], :] = value[:, j * LANES:(j + 1) * LANES]
        copy = remote(out_core[p], in_core[p], core_send.at[p], core_recv.at[p], sibling)
        copy.start()
        to_core.append(copy)
    for p in range(PARTS):
        value = term(core, p)
        for j in range(COLS):
            own_term[p][j * PART[p]:(j + 1) * PART[p], :] = value[:, j * LANES:(j + 1) * LANES]

    pending = list(to_core)

    def start_all(stage, p, axis, src_of, dst_of):
        copies = []
        for by in far_first(SIZE[axis]):
            copy = remote(
                src_of(by), dst_of(by), stage_send.at[stage, p, by], stage_recv.at[stage, p, by], shifted(me, axis, by)
            )
            copy.start()
            copies.append(copy)
        pending.extend(copies)
        return copies

    def slot(axis, rows):
        return pl.ds(pl.multiple_of(place(me, axis) * rows, TILE), rows)

    def slot_of(axis, by, rows):
        return pl.ds(pl.multiple_of(lax.rem(place(me, axis) + by, SIZE[axis]) * rows, TILE), rows)

    arrivals = [None] * PARTS
    for p, (axis, _, _) in enumerate(ORDERS):
        to_core[p].wait_recv()
        s1_out[p][:FLAT[p], :] = (own_term[p][...] + in_core[p][...].astype(F32)).astype(BF16)
        if FULL1[p] > FLAT[p]:
            s1_out[p][FLAT[p]:, :] = jnp.zeros((FULL1[p] - FLAT[p], LANES), BF16)
        arrivals[p] = start_all(
            0, p, axis, lambda by: s1_out[p].at[slot_of(axis, by, SUM1[p])], lambda by: s1_in[p].at[by]
        )

    cgrad[...] = lax.dot_general(
        dh[...], projection[...], (((1,), (1,)), ((), ())), preferred_element_type=F32
    ).astype(BF16)
    store = pltpu.make_async_copy(cgrad, cgrad_ref, last_sem.at[0])
    store.start()

    for p, (axis1, axis2, _) in enumerate(ORDERS):
        for copy in arrivals[p]:
            copy.wait_recv()
        value = s1_out[p][slot(axis1, SUM1[p]), :].astype(F32)
        for by in range(1, SIZE[axis1]):
            value += s1_in[p][by].astype(F32)
        s2_out[p][:SUM1[p], :] = value.astype(BF16)
        if FULL2[p] > SUM1[p]:
            s2_out[p][SUM1[p]:, :] = jnp.zeros((FULL2[p] - SUM1[p], LANES), BF16)
        arrivals[p] = start_all(
            1, p, axis2, lambda by: s2_out[p].at[slot_of(axis2, by, SUM2[p])], lambda by: s2_in[p].at[by]
        )

    for p, (_, axis2, axis3) in enumerate(ORDERS):
        for copy in arrivals[p]:
            copy.wait_recv()
        value = s2_out[p][slot(axis2, SUM2[p]), :].astype(F32)
        for by in range(1, SIZE[axis2]):
            value += s2_in[p][by].astype(F32)
        here = place(me, axis3)
        s3_in[p][here] = value.astype(BF16)
        arrivals[p] = start_all(2, p, axis3, lambda by: s3_in[p].at[here], lambda by: s3_in[p].at[here])

    devices = 1
    for size in SIZE.values():
        devices *= size

    for p, (_, axis2, axis3) in enumerate(ORDERS):
        for copy in arrivals[p]:
            copy.wait_recv()
        value = s3_in[p][0].astype(F32)
        for k in range(1, SIZE[axis3]):
            value += s3_in[p][k].astype(F32)
        mine = slot(axis2, SUM2[p])
        gather2[p][mine, :] = (value / devices).astype(BF16)
        arrivals[p] = start_all(3, p, axis2, lambda by: gather2[p].at[mine], lambda by: gather2[p].at[mine])

    for p, (axis1, _, _) in enumerate(ORDERS):
        for copy in arrivals[p]:
            copy.wait_recv()
        mine = slot(axis1, SUM1[p])
        gather1[p][mine, :] = gather2[p][:SUM1[p], :]
        arrivals[p] = start_all(4, p, axis1, lambda by: gather1[p].at[mine], lambda by: gather1[p].at[mine])

    writes = []
    for p in range(PARTS):
        for copy in arrivals[p]:
            copy.wait_recv()
        for j in range(COLS):
            result[p][:, j * LANES:(j + 1) * LANES] = gather1[p][j * PART[p]:(j + 1) * PART[p], :]
        dst = pgrad_ref.at[pl.ds(pl.multiple_of(core * HALF + FIRST[p], TILE), PART[p])]
        copy = remote(result[p], dst, last_send.at[p], last_recv.at[p], sibling)
        copy.start()
        write = pltpu.make_async_copy(result[p], dst, last_sem.at[1 + p])
        write.start()
        writes.append((copy, write))
    for copy, write in writes:
        copy.wait()
        write.wait()

    store.wait()
    for swap in [*swaps, swap_x, swap_core, *pending]:
        swap.wait_send()


def local(video_emb, captions, projection, labels, log_scale, bias):
    dma = pltpu.SemaphoreType.DMA
    vmem = pltpu.VMEM

    def each(shape_of, dtype=BF16):
        return [vmem(shape_of(p), dtype) for p in range(PARTS)]

    return pl.pallas_call(
        kernel,
        out_shape=(
            jax.ShapeDtypeStruct((ROWS, D), BF16),
            jax.ShapeDtypeStruct((D, E), BF16),
        ),
        in_specs=[pl.BlockSpec(memory_space=pltpu.HBM)] * 3
        + [pl.BlockSpec(memory_space=pltpu.VMEM)]
        + [pl.BlockSpec(memory_space=pltpu.SMEM)] * 2,
        out_specs=[pl.BlockSpec(memory_space=pltpu.HBM)] * 2,
        scratch_shapes=[
            vmem((ROWS, E), BF16),
            vmem((ROWS, D), BF16),
            vmem((D, E), BF16),
            vmem((D, ROWS), BF16),
            vmem((ROWS, E), F32),
            vmem((ROWS, E), BF16),
            vmem((ROWS, 1), F32),
            vmem((ROWS, E), F32),
            vmem((ROWS, E), BF16),
            vmem((ROWS, D), BF16),
            vmem((ROWS, E), BF16),
            vmem((ROWS, E), BF16),
            vmem((CHUNKS, 2 * CHUNK, E), BF16),
            each(lambda p: (FLAT[p], LANES)),
            each(lambda p: (FLAT[p], LANES)),
            each(lambda p: (FLAT[p], LANES), F32),
            each(lambda p: (FULL1[p], LANES)),
            each(lambda p: (SIZE[ORDERS[p][0]], SUM1[p], LANES)),
            each(lambda p: (FULL2[p], LANES)),
            each(lambda p: (SIZE[ORDERS[p][1]], SUM2[p], LANES)),
            each(lambda p: (SIZE[ORDERS[p][2]], SUM2[p], LANES)),
            each(lambda p: (FULL2[p], LANES)),
            each(lambda p: (FULL1[p], LANES)),
            each(lambda p: (PART[p], E)),
            dma((3,)),
            dma((4, CHUNKS)),
            dma((4, CHUNKS)),
            dma((PARTS,)),
            dma((PARTS,)),
            dma((5, PARTS, 8)),
            dma((5, PARTS, 8)),
            dma((1 + PARTS,)),
            dma((PARTS,)),
            dma((PARTS,)),
            pltpu.SemaphoreType.REGULAR,
        ],
        compiler_params=pltpu.CompilerParams(
            collective_id=0, has_side_effects=True, vmem_limit_bytes=63 << 20
        ),
    )(video_emb, captions, projection, labels, log_scale, bias)


def solution(mesh):
    return jax.shard_map(
        local,
        mesh=mesh,
        in_specs=(P("dp", None), P("dp", None), P(), P("dp"), P(), P()),
        out_specs=(P("dp", None), P()),
        check_vma=False,
    )
```

time: 84.4 us -> 81.1 us (0.961)
  local copies, waits for them, and re-layouts: 6.28 us -> 3.37 us
    unnamed x8 -> x4, local copies, waits for them, and re-layouts: 5.59 us -> 3.37 us
where the time goes in v2:
time: 81.1 us; the launch traced here: 80.9 us
  Pallas kernels  75.6 us (93%)
  local copies, waits for them, and re-layouts  3.37 us (4%)
  between operations  1.94 us (2%)
    pallas_call x1, Pallas kernels, local(): pl.pallas_call(kernel, out_shape=(jax.ShapeDtypeStruct((ROWS, D), BF16),...  75.6 us
    unnamed x4, local copies, waits for them, and re-layouts  3.37 us

profile of v2, /device:TPU:1, one launch (start us, length us, event | category | flops | bytes accessed | tf_op | source)
XLA Modules:
  0.0 80.9 jit_solution(6107835011009274316)
XLA Ops:
  1.9 75.6 %shard_map.77 = (bf16[384,1152]{1,0:T(8,128)(2,1)}, bf16[1152,640]{1,0:T(8,128)(2,1)}) custom-call(bf16[384,640]{1,0:T(8,128)(2,1)} %video_ref.1, bf16[384,1152]{1,0:T(8,128)(2,1)} %captions_ref.1, bf16[1152,640]{1,0:T(8,128)(2,1)} %projection_ref.1, s32[384]{0:T(512)} %labels_ref.1, f32[1]{0:T(128)S(6)} %copy.10.log_scale_ref, f32[1]{0:T(128)S(6)} %copy.11.bias_ref), custom_call_target="tpu_custom_call" | custom-call | tf_op jit(solution)/shard_map/pallas_call | solution.py:281
  77.5 0.0 copy-start
  77.6 2.3 %copy.12 = bf16[384,1152]{1,0:T(8,128)(2,1)} copy(bf16[384,1152]{1,0:T(8,128)(2,1)} %get-tuple-element.4) | data formatting | bytes 1769472
  79.8 0.0 copy-done
  79.8 1.1 %copy.13 = bf16[1152,640]{1,0:T(8,128)(2,1)} copy(bf16[1152,640]{1,0:T(8,128)(2,1)S(1)} %copy-done) | data formatting | bytes 2949120
Async XLA Ops:
  77.5 2.3 %copy-start = (bf16[1152,640]{1,0:T(8,128)(2,1)S(1)}, bf16[1152,640]{1,0:T(8,128)(2,1)}, u32[]{:S(2)}) copy-start(bf16[1152,640]{1,0:T(8,128)(2,1)} %get-tuple-element.5) | copy-start | bytes 4423684

commit v3 on v2

--- a/solution.py
+++ b/solution.py
@@ -62,14 +62,18 @@
     return sorted(range(1, size), key=lambda by: -min(by, size - by))
 
 
+def far_last(size):
+    return far_first(size)[::-1]
+
+
 def kernel(
     video_ref, captions_ref, projection_ref, labels_ref, log_scale_ref, bias_ref,
     cgrad_ref, pgrad_ref,
-    video, captions, projection, flipped, zf, zc, inv, dz, dh, cgrad,
+    video, captions, projection, flipped, labels, zf, zc, inv, dz, dh,
     own_core, own_x, pool,
-    out_core, in_core, own_term, s1_out, s1_in, s2_out, s2_in, s3_in, gather2, gather1, result,
+    out_core, in_core, own_term, s1_out, s1_in, s2_out, s2_in, s3_in, gather2, gather1, other1,
     load_sem, swap_send, swap_recv, core_send, core_recv,
-    stage_send, stage_recv, last_sem, last_send, last_recv, round_sem,
+    stage_send, stage_recv, last_send, last_recv, round_sem,
 ):
     me = lax.axis_index("dp")
     core = place(me, "core")
@@ -79,6 +83,7 @@
         pltpu.make_async_copy(video_ref, video, load_sem.at[0]),
         pltpu.make_async_copy(captions_ref, captions, load_sem.at[1]),
         pltpu.make_async_copy(projection_ref, projection, load_sem.at[2]),
+        pltpu.make_async_copy(labels_ref, labels, load_sem.at[3]),
     ]
     for load in loads:
         load.start()
@@ -116,6 +121,7 @@
 
     loads[1].wait()
     loads[2].wait()
+    loads[3].wait()
     hidden = jnp.dot(captions[...], projection[...], preferred_element_type=F32)
     inverse = lax.rsqrt(jnp.sum(hidden * hidden, axis=-1, keepdims=True) + 1e-06)
     unit = hidden * inverse
@@ -137,7 +143,7 @@
 
     row = lax.broadcasted_iota(jnp.int32, (ROWS, ROWS), 0)
     column = lax.broadcasted_iota(jnp.int32, (ROWS, ROWS), 1)
-    sign = jnp.where((row == column) & (labels_ref[...].reshape(1, ROWS) == 1), -1.0, 1.0).astype(F32)
+    sign = jnp.where((row == column) & (labels[...].reshape(1, ROWS) == 1), -1.0, 1.0).astype(F32)
     dz[...] = pairing(video[...], sign)
     flipped[...] = captions[...].T
     pl.semaphore_wait(round_sem, len(neighbours))
@@ -200,11 +206,9 @@
             0, p, axis, lambda by: s1_out[p].at[slot_of(axis, by, SUM1[p])], lambda by: s1_in[p].at[by]
         )
 
-    cgrad[...] = lax.dot_general(
+    cgrad_ref[...] = lax.dot_general(
         dh[...], projection[...], (((1,), (1,)), ((), ())), preferred_element_type=F32
     ).astype(BF16)
-    store = pltpu.make_async_copy(cgrad, cgrad_ref, last_sem.at[0])
-    store.start()
 
     for p, (axis1, axis2, _) in enumerate(ORDERS):
         for copy in arrivals[p]:
@@ -243,32 +247,52 @@
         gather2[p][mine, :] = (value / devices).astype(BF16)
         arrivals[p] = start_all(3, p, axis2, lambda by: gather2[p].at[mine], lambda by: gather2[p].at[mine])
 
+    crossings = [[] for _ in range(PARTS)]
+
+    def across(p, by):
+        axis = ORDERS[p][0]
+        rows = slot_of(axis, SIZE[axis] - by, SUM1[p])
+        copy = remote(gather1[p].at[rows], other1[p].at[rows], last_send.at[p, by], last_recv.at[p, by], sibling)
+        copy.start()
+        crossings[p].append(copy)
+
     for p, (axis1, _, _) in enumerate(ORDERS):
         for copy in arrivals[p]:
             copy.wait_recv()
         mine = slot(axis1, SUM1[p])
         gather1[p][mine, :] = gather2[p][:SUM1[p], :]
         arrivals[p] = start_all(4, p, axis1, lambda by: gather1[p].at[mine], lambda by: gather1[p].at[mine])
-
-    writes = []
+        across(p, 0)
+
+    for p, (axis1, _, _) in enumerate(ORDERS):
+        for by, copy in zip(far_last(SIZE[axis1]), reversed(arrivals[p])):
+            copy.wait_recv()
+            across(p, by)
     for p in range(PARTS):
-        for copy in arrivals[p]:
-            copy.wait_recv()
         for j in range(COLS):
-            result[p][:, j * LANES:(j + 1) * LANES] = gather1[p][j * PART[p]:(j + 1) * PART[p], :]
-        dst = pgrad_ref.at[pl.ds(pl.multiple_of(core * HALF + FIRST[p], TILE), PART[p])]
-        copy = remote(result[p], dst, last_send.at[p], last_recv.at[p], sibling)
-        copy.start()
-        write = pltpu.make_async_copy(result[p], dst, last_sem.at[1 + p])
-        write.start()
-        writes.append((copy, write))
-    for copy, write in writes:
-        copy.wait()
-        write.wait()
-
-    store.wait()
+            rows = pl.ds(pl.multiple_of(core * HALF + FIRST[p], TILE), PART[p])
+            pgrad_ref[rows, j * LANES:(j + 1) * LANES] = gather1[p][j * PART[p]:(j + 1) * PART[p], :]
+    for p in range(PARTS):
+        for copy in crossings[p]:
+            copy.wait_recv()
+        for j in range(COLS):
+            rows = pl.ds(pl.multiple_of((1 - core) * HALF + FIRST[p], TILE), PART[p])
+            pgrad_ref[rows, j * LANES:(j + 1) * LANES] = other1[p][j * PART[p]:(j + 1) * PART[p], :]
+        pending.extend(crossings[p])
+
     for swap in [*swaps, swap_x, swap_core, *pending]:
         swap.wait_send()
+
+
+def hand_over(cgrad_ref, pgrad_ref, cgrad_out, pgrad_out, sem):
+    copies = [
+        pltpu.make_async_copy(cgrad_ref, cgrad_out, sem.at[0]),
+        pltpu.make_async_copy(pgrad_ref, pgrad_out, sem.at[1]),
+    ]
+    for copy in copies:
+        copy.start()
+    for copy in copies:
+        copy.wait()
 
 
 def local(video_emb, captions, projection, labels, log_scale, bias):
@@ -278,27 +302,27 @@
     def each(shape_of, dtype=BF16):
         return [vmem(shape_of(p), dtype) for p in range(PARTS)]
 
-    return pl.pallas_call(
+    held = [pltpu.with_memory_space_constraint(x, pltpu.HBM) for x in (video_emb, captions, projection, labels)]
+    cgrad, pgrad = pl.pallas_call(
         kernel,
         out_shape=(
             jax.ShapeDtypeStruct((ROWS, D), BF16),
             jax.ShapeDtypeStruct((D, E), BF16),
         ),
-        in_specs=[pl.BlockSpec(memory_space=pltpu.HBM)] * 3
-        + [pl.BlockSpec(memory_space=pltpu.VMEM)]
+        in_specs=[pl.BlockSpec(memory_space=pl.ANY)] * 4
         + [pl.BlockSpec(memory_space=pltpu.SMEM)] * 2,
-        out_specs=[pl.BlockSpec(memory_space=pltpu.HBM)] * 2,
+        out_specs=[pl.BlockSpec(memory_space=pltpu.VMEM)] * 2,
         scratch_shapes=[
             vmem((ROWS, E), BF16),
             vmem((ROWS, D), BF16),
             vmem((D, E), BF16),
             vmem((D, ROWS), BF16),
+            vmem((ROWS,), jnp.int32),
             vmem((ROWS, E), F32),
             vmem((ROWS, E), BF16),
             vmem((ROWS, 1), F32),
             vmem((ROWS, E), F32),
             vmem((ROWS, E), BF16),
-            vmem((ROWS, D), BF16),
             vmem((ROWS, E), BF16),
             vmem((ROWS, E), BF16),
             vmem((CHUNKS, 2 * CHUNK, E), BF16),
@@ -312,23 +336,32 @@
             each(lambda p: (SIZE[ORDERS[p][2]], SUM2[p], LANES)),
             each(lambda p: (FULL2[p], LANES)),
             each(lambda p: (FULL1[p], LANES)),
-            each(lambda p: (PART[p], E)),
-            dma((3,)),
+            each(lambda p: (FULL1[p], LANES)),
+            dma((4,)),
             dma((4, CHUNKS)),
             dma((4, CHUNKS)),
             dma((PARTS,)),
             dma((PARTS,)),
             dma((5, PARTS, 8)),
             dma((5, PARTS, 8)),
-            dma((1 + PARTS,)),
-            dma((PARTS,)),
-            dma((PARTS,)),
+            dma((PARTS, 8)),
+            dma((PARTS, 8)),
             pltpu.SemaphoreType.REGULAR,
         ],
         compiler_params=pltpu.CompilerParams(
-            collective_id=0, has_side_effects=True, vmem_limit_bytes=63 << 20
+            collective_id=0, has_side_effects=True, vmem_limit_bytes=40 << 20
         ),
-    )(video_emb, captions, projection, labels, log_scale, bias)
+    )(*held, log_scale, bias)
+    return pl.pallas_call(
+        hand_over,
+        out_shape=(
+            jax.ShapeDtypeStruct((ROWS, D), BF16),
+            jax.ShapeDtypeStruct((D, E), BF16),
+        ),
+        in_specs=[pl.BlockSpec(memory_space=pl.ANY)] * 2,
+        out_specs=[pl.BlockSpec(memory_space=pl.ANY)] * 2,
+        scratch_shapes=[dma((2,))],
+    )(cgrad, pgrad)
 
 
 def solution(mesh):

time: 81.1 us -> 151 us (1.86)
  Pallas kernels: 75.6 us -> 147 us
    pallas_call x0 -> x1, Pallas kernels: none -> 72.6 us  [local(): pl.pallas_call(hand_over, out_shape=(jax.ShapeDtypeStruct((ROWS, D), BF16...]
where the time goes in v3:
time: 151 us
  Pallas kernels  147 us (97%)
  local copies, waits for them, and re-layouts  2.05 us (1%)
  between operations  1.94 us (1%)
    pallas_call x1, Pallas kernels, local(): pl.pallas_call(kernel, out_shape=(jax.ShapeDtypeStruct((ROWS, D), BF16),...  74.7 us
    pallas_call x1, Pallas kernels, local(): pl.pallas_call(hand_over, out_shape=(jax.ShapeDtypeStruct((ROWS, D), BF16...  72.6 us

profile of v3, /device:TPU:1, one launch (start us, length us, event | category | flops | bytes accessed | tf_op | source)
XLA Modules:
  0.0 151.3 jit_solution(7586554805235675071)
XLA Ops:
  1.9 74.7 %shard_map.77 = (bf16[384,1152]{1,0:T(8,128)(2,1)S(1)}, bf16[1152,640]{1,0:T(8,128)(2,1)S(1)}) custom-call(bf16[384,640]{1,0:T(8,128)(2,1)} %video_ref.1, bf16[384,1152]{1,0:T(8,128)(2,1)} %captions_ref.1, bf16[1152,640]{1,0:T(8,128)(2,1)} %projection_ref.1, s32[384]{0:T(512)} %labels_ref.1, f32[1]{0:T(128)S(6)} %copy.8.log_scale_ref, f32[1]{0:T(128)S(6)} %copy.9.bias_ref), custom_call_target="tpu_custom_call" | custom-call | tf_op jit(solution)/shard_map/pallas_call | solution.py:306
  76.6 0.0 copy-start
  76.6 1.1 copy-done
  77.8 0.0 copy-start.1
  77.8 0.9 copy-done.1
  78.7 72.6 %shard_map.78 = (bf16[384,1152]{1,0:T(8,128)(2,1)}, bf16[1152,640]{1,0:T(8,128)(2,1)}) custom-call(bf16[384,1152]{1,0:T(8,128)(2,1)} %copy-done.1, bf16[1152,640]{1,0:T(8,128)(2,1)} %copy-done), custom_call_target="tpu_custom_call" | custom-call | tf_op jit(solution)/shard_map/pallas_call | solution.py:355
Async XLA Ops:
  76.6 1.1 copy-start
  77.8 0.9 copy-start.1

commit v4 on v3

--- a/solution.py
+++ b/solution.py
@@ -24,10 +24,11 @@
 COLS = E // LANES
 TILE = 16
 
-ORDERS = (("y", "z", "x"), ("z", "x", "y"), ("x", "y", "z"))
-PART = (144, 144, 288)
-FIRST = (0, 144, 288)
+ORDERS = (("x", "y", "z"), ("y", "z", "x"), ("z", "x", "y"))
+PART = (288, 144, 144)
+FIRST = (0, 288, 432)
 PARTS = len(ORDERS)
+PIECES = 3
 
 
 def up(value, multiple):
@@ -177,7 +178,15 @@
         for j in range(COLS):
             own_term[p][j * PART[p]:(j + 1) * PART[p], :] = value[:, j * LANES:(j + 1) * LANES]
 
-    pending = list(to_core)
+    pending = [*swaps, swap_x, swap_core, *to_core]
+
+    def sent():
+        for copy in pending:
+            copy.wait_send()
+        pending[:] = started
+        started.clear()
+
+    started = []
 
     def start_all(stage, p, axis, src_of, dst_of):
         copies = []
@@ -187,7 +196,7 @@
             )
             copy.start()
             copies.append(copy)
-        pending.extend(copies)
+        started.extend(copies)
         return copies
 
     def slot(axis, rows):
@@ -210,6 +219,8 @@
         dh[...], projection[...], (((1,), (1,)), ((), ())), preferred_element_type=F32
     ).astype(BF16)
 
+    sent()
+
     for p, (axis1, axis2, _) in enumerate(ORDERS):
         for copy in arrivals[p]:
             copy.wait_recv()
@@ -223,6 +234,8 @@
             1, p, axis2, lambda by: s2_out[p].at[slot_of(axis2, by, SUM2[p])], lambda by: s2_in[p].at[by]
         )
 
+    sent()
+
     for p, (_, axis2, axis3) in enumerate(ORDERS):
         for copy in arrivals[p]:
             copy.wait_recv()
@@ -237,6 +250,8 @@
     for size in SIZE.values():
         devices *= size
 
+    sent()
+
     for p, (_, axis2, axis3) in enumerate(ORDERS):
         for copy in arrivals[p]:
             copy.wait_recv()
@@ -256,6 +271,8 @@
         copy.start()
         crossings[p].append(copy)
 
+    sent()
+
     for p, (axis1, _, _) in enumerate(ORDERS):
         for copy in arrivals[p]:
             copy.wait_recv()
@@ -263,6 +280,8 @@
         gather1[p][mine, :] = gather2[p][:SUM1[p], :]
         arrivals[p] = start_all(4, p, axis1, lambda by: gather1[p].at[mine], lambda by: gather1[p].at[mine])
         across(p, 0)
+
+    sent()
 
     for p, (axis1, _, _) in enumerate(ORDERS):
         for by, copy in zip(far_last(SIZE[axis1]), reversed(arrivals[p])):
@@ -278,17 +297,19 @@
         for j in range(COLS):
             rows = pl.ds(pl.multiple_of((1 - core) * HALF + FIRST[p], TILE), PART[p])
             pgrad_ref[rows, j * LANES:(j + 1) * LANES] = other1[p][j * PART[p]:(j + 1) * PART[p], :]
-        pending.extend(crossings[p])
-
-    for swap in [*swaps, swap_x, swap_core, *pending]:
-        swap.wait_send()
+        started.extend(crossings[p])
+
+    sent()
+    sent()
 
 
 def hand_over(cgrad_ref, pgrad_ref, cgrad_out, pgrad_out, sem):
-    copies = [
-        pltpu.make_async_copy(cgrad_ref, cgrad_out, sem.at[0]),
-        pltpu.make_async_copy(pgrad_ref, pgrad_out, sem.at[1]),
-    ]
+    copies = []
+    for source, target in ((cgrad_ref, cgrad_out), (pgrad_ref, pgrad_out)):
+        rows = source.shape[0] // PIECES
+        for k in range(PIECES):
+            piece = pl.ds(k * rows, rows)
+            copies.append(pltpu.make_async_copy(source.at[piece], target.at[piece], sem.at[len(copies)]))
     for copy in copies:
         copy.start()
     for copy in copies:
@@ -360,7 +381,8 @@
         ),
         in_specs=[pl.BlockSpec(memory_space=pl.ANY)] * 2,
         out_specs=[pl.BlockSpec(memory_space=pl.ANY)] * 2,
-        scratch_shapes=[dma((2,))],
+        scratch_shapes=[dma((2 * PIECES,))],
+        compiler_params=pltpu.CompilerParams(vmem_limit_bytes=1 << 20),
     )(cgrad, pgrad)
 
 

time: 151 us -> 77.8 us (0.52)
  Pallas kernels: 147 us -> 75.7 us
  local copies, waits for them, and re-layouts: 2.05 us -> 0 us
    pallas_call x1, Pallas kernels: 72.6 us -> 1.45 us  [local(): pl.pallas_call(hand_over, out_shape=(jax.ShapeDtypeStruct((ROWS, D), BF16...]
    unnamed x4 -> x0, local copies, waits for them, and re-layouts: 2.05 us -> none
where the time goes in v4:
time: 77.8 us; the launch traced here: 77.6 us
  Pallas kernels  75.7 us (97%)
  between operations  1.93 us (2%)
    pallas_call x1, Pallas kernels, local(): pl.pallas_call(kernel, out_shape=(jax.ShapeDtypeStruct((ROWS, D), BF16),...  74.2 us

profile of v4, /device:TPU:1, one launch (start us, length us, event | category | flops | bytes accessed | tf_op | source)
XLA Modules:
  0.0 77.6 jit_solution(6747838507884519158)
XLA Ops:
  1.9 74.2 %shard_map.77 = (bf16[384,1152]{1,0:T(8,128)(2,1)S(1)}, bf16[1152,640]{1,0:T(8,128)(2,1)S(1)}) custom-call(bf16[384,640]{1,0:T(8,128)(2,1)} %video_ref.1, bf16[384,1152]{1,0:T(8,128)(2,1)} %captions_ref.1, bf16[1152,640]{1,0:T(8,128)(2,1)} %projection_ref.1, s32[384]{0:T(512)} %labels_ref.1, f32[1]{0:T(128)S(6)} %copy.8.log_scale_ref, f32[1]{0:T(128)S(6)} %copy.9.bias_ref), custom_call_target="tpu_custom_call" | custom-call | tf_op jit(solution)/shard_map/pallas_call | solution.py:327
  76.2 1.4 %shard_map.78 = (bf16[384,1152]{1,0:T(8,128)(2,1)}, bf16[1152,640]{1,0:T(8,128)(2,1)}) custom-call(bf16[384,1152]{1,0:T(8,128)(2,1)S(1)} %get-tuple-element.4.cgrad_ref, bf16[1152,640]{1,0:T(8,128)(2,1)S(1)} %get-tuple-element.5.pgrad_ref), custom_call_target="tpu_custom_call" | custom-call | tf_op jit(solution)/shard_map/pallas_call | solution.py:376

commit v5 on v4

--- a/solution.py
+++ b/solution.py
@@ -19,15 +19,18 @@
 D = 1152
 HALF = D // 2
 CHUNKS = 3
-CHUNK = ROWS // CHUNKS
+CHUNK = ROWS // (2 * CHUNKS)
+NEAR, REST = 1, 3
+WAYS = (("y", 1), ("y", -1), ("z", 1), ("z", -1))
 LANES = 128
 COLS = E // LANES
 TILE = 16
 
-ORDERS = (("x", "y", "z"), ("y", "z", "x"), ("z", "x", "y"))
-PART = (288, 144, 144)
-FIRST = (0, 288, 432)
+ORDERS = (("x", "y", "z"), ("y", "x", "z"), ("z", "x", "y"))
+PART = (256, 160, 160)
+FIRST = (0, 256, 416)
 PARTS = len(ORDERS)
+READY = (1, 2, 0)
 PIECES = 3
 
 
@@ -71,9 +74,9 @@
     video_ref, captions_ref, projection_ref, labels_ref, log_scale_ref, bias_ref,
     cgrad_ref, pgrad_ref,
     video, captions, projection, flipped, labels, zf, zc, inv, dz, dh,
-    own_core, own_x, pool,
+    own_core, own_x, relay, pool,
     out_core, in_core, own_term, s1_out, s1_in, s2_out, s2_in, s3_in, gather2, gather1, other1,
-    load_sem, swap_send, swap_recv, core_send, core_recv,
+    load_sem, hop_send, hop_recv, swap_send, swap_recv, core_send, core_recv,
     stage_send, stage_recv, last_send, last_recv, round_sem,
 ):
     me = lax.axis_index("dp")
@@ -90,28 +93,35 @@
         load.start()
 
     barrier = pltpu.get_barrier_semaphore()
-    greeted = [(axis, SIZE[axis] // 2) for axis in ("y", "z", "x")]
-    greeted += [(axis, by) for axis in ("y", "z", "x") for by in (1, -1)] + [("core", 1)]
+    greeted = [(axis, way * by) for by in sorted({1, NEAR, REST}) for axis, way in WAYS]
+    greeted += [("x", 2), ("x", 1), ("x", -1), ("core", 1)]
     for axis, by in greeted:
         pl.semaphore_signal(barrier, inc=1, device_id=(shifted(me, axis, by),), device_id_type=MESH)
     pl.semaphore_wait(barrier, len(greeted))
     loads[0].wait()
 
-    swaps = []
+    hops = []
     for q in range(CHUNKS):
-        rows = pl.ds(q * CHUNK, CHUNK)
-        for w, axis in enumerate(("y", "z")):
-            swap = remote(
-                video.at[rows], pool.at[q, pl.ds(w * CHUNK, CHUNK)], swap_send.at[w, q], swap_recv.at[w, q],
-                shifted(me, axis, SIZE[axis] // 2),
+        for w, (axis, way) in enumerate(WAYS):
+            rows = pl.ds(((0 if way > 0 else CHUNKS) + q) * CHUNK, CHUNK)
+            first = remote(
+                video.at[rows], relay.at[q, w], hop_send.at[q, w, 0], hop_recv.at[q, w, 0], shifted(me, axis, way * NEAR)
             )
-            swap.start()
-            swaps.append(swap)
-        if q == 0:
-            swap_x = remote(video, own_x, swap_send.at[2, 0], swap_recv.at[2, 0], shifted(me, "x", SIZE["x"] // 2))
-            swap_x.start()
-            swap_core = remote(video, own_core, swap_send.at[3, 0], swap_recv.at[3, 0], sibling)
-            swap_core.start()
+            second = remote(
+                relay.at[q, w], pool.at[q, pl.ds(w * CHUNK, CHUNK)], hop_send.at[q, w, 1], hop_recv.at[q, w, 1],
+                shifted(me, axis, way * REST),
+            )
+            first.start()
+            hops.append((first, second))
+    swap_x = remote(video, own_x, swap_send.at[0], swap_recv.at[0], shifted(me, "x", 2))
+    swap_x.start()
+    swap_core = remote(video, own_core, swap_send.at[1], swap_recv.at[1], sibling)
+    swap_core.start()
+
+    def pass_on(q):
+        for first, second in hops[q * len(WAYS):(q + 1) * len(WAYS)]:
+            first.wait_recv()
+            second.start()
 
     neighbours = [("y", 1), ("y", -1), ("z", 1), ("z", -1)]
     for axis, by in neighbours:
@@ -142,10 +152,13 @@
             weight = sign / (1.0 + jnp.exp(-sign * logits))
         return jnp.dot(weight.astype(BF16), zv, preferred_element_type=F32)
 
+    pass_on(0)
     row = lax.broadcasted_iota(jnp.int32, (ROWS, ROWS), 0)
     column = lax.broadcasted_iota(jnp.int32, (ROWS, ROWS), 1)
     sign = jnp.where((row == column) & (labels[...].reshape(1, ROWS) == 1), -1.0, 1.0).astype(F32)
     dz[...] = pairing(video[...], sign)
+    for q in range(1, CHUNKS):
+        pass_on(q)
     flipped[...] = captions[...].T
     pl.semaphore_wait(round_sem, len(neighbours))
     swap_core.wait_recv()
@@ -153,11 +166,12 @@
     swap_x.wait_recv()
     dz[...] += pairing(own_x[...])
     for q in range(CHUNKS):
-        for swap in swaps[2 * q:2 * q + 2]:
-            swap.wait_recv()
-        dz[...] += pairing(pool[q])
-
-    total = scale * dz[...]
+        for _, second in hops[q * len(WAYS):(q + 1) * len(WAYS)]:
+            second.wait_recv()
+        if q < CHUNKS - 1:
+            dz[...] += pairing(pool[q])
+
+    total = scale * (dz[...] + pairing(pool[CHUNKS - 1]))
     along = jnp.sum(zf[...] * total, axis=-1, keepdims=True)
     dh[...] = (inv[...] * (total - zf[...] * along)).astype(BF16)
 
@@ -178,7 +192,7 @@
         for j in range(COLS):
             own_term[p][j * PART[p]:(j + 1) * PART[p], :] = value[:, j * LANES:(j + 1) * LANES]
 
-    pending = [*swaps, swap_x, swap_core, *to_core]
+    pending = [copy for pair in hops for copy in pair] + [swap_x, swap_core, *to_core]
 
     def sent():
         for copy in pending:
@@ -273,25 +287,28 @@
 
     sent()
 
-    for p, (axis1, _, _) in enumerate(ORDERS):
+    for p in READY:
+        axis1 = ORDERS[p][0]
         for copy in arrivals[p]:
             copy.wait_recv()
         mine = slot(axis1, SUM1[p])
         gather1[p][mine, :] = gather2[p][:SUM1[p], :]
         arrivals[p] = start_all(4, p, axis1, lambda by: gather1[p].at[mine], lambda by: gather1[p].at[mine])
+
+    sent()
+
+    for p in READY:
         across(p, 0)
-
-    sent()
-
-    for p, (axis1, _, _) in enumerate(ORDERS):
+    for p in READY:
+        axis1 = ORDERS[p][0]
         for by, copy in zip(far_last(SIZE[axis1]), reversed(arrivals[p])):
             copy.wait_recv()
             across(p, by)
-    for p in range(PARTS):
+    for p in READY:
         for j in range(COLS):
             rows = pl.ds(pl.multiple_of(core * HALF + FIRST[p], TILE), PART[p])
             pgrad_ref[rows, j * LANES:(j + 1) * LANES] = gather1[p][j * PART[p]:(j + 1) * PART[p], :]
-    for p in range(PARTS):
+    for p in READY:
         for copy in crossings[p]:
             copy.wait_recv()
         for j in range(COLS):
@@ -346,7 +363,8 @@
             vmem((ROWS, E), BF16),
             vmem((ROWS, E), BF16),
             vmem((ROWS, E), BF16),
-            vmem((CHUNKS, 2 * CHUNK, E), BF16),
+            vmem((CHUNKS, len(WAYS), CHUNK, E), BF16),
+            vmem((CHUNKS, len(WAYS) * CHUNK, E), BF16),
             each(lambda p: (FLAT[p], LANES)),
             each(lambda p: (FLAT[p], LANES)),
             each(lambda p: (FLAT[p], LANES), F32),
@@ -359,8 +377,10 @@
             each(lambda p: (FULL1[p], LANES)),
             each(lambda p: (FULL1[p], LANES)),
             dma((4,)),
-            dma((4, CHUNKS)),
-            dma((4, CHUNKS)),
+            dma((CHUNKS, len(WAYS), 2)),
+            dma((CHUNKS, len(WAYS), 2)),
+            dma((2,)),
+            dma((2,)),
             dma((PARTS,)),
             dma((PARTS,)),
             dma((5, PARTS, 8)),

time: 77.8 us -> 76.9 us (0.988)
  Pallas kernels: 75.7 us -> 74.8 us
    pallas_call x1, Pallas kernels: 74.2 us -> 73.3 us  [local(): pl.pallas_call(kernel, out_shape=(jax.ShapeDtypeStruct((ROWS, D), BF16),...]
where the time goes in v5:
time: 76.9 us; the launch traced here: 76.7 us
  Pallas kernels  74.8 us (97%)
  between operations  1.93 us (3%)
    pallas_call x1, Pallas kernels, local(): pl.pallas_call(kernel, out_shape=(jax.ShapeDtypeStruct((ROWS, D), BF16),...  73.3 us

profile of v5, /device:TPU:1, one launch (start us, length us, event | category | flops | bytes accessed | tf_op | source)
XLA Modules:
  0.0 76.7 jit_solution(5350298487696912004)
XLA Ops:
  1.9 73.3 %shard_map.77 = (bf16[384,1152]{1,0:T(8,128)(2,1)S(1)}, bf16[1152,640]{1,0:T(8,128)(2,1)S(1)}) custom-call(bf16[384,640]{1,0:T(8,128)(2,1)} %video_ref.1, bf16[384,1152]{1,0:T(8,128)(2,1)} %captions_ref.1, bf16[1152,640]{1,0:T(8,128)(2,1)} %projection_ref.1, s32[384]{0:T(512)} %labels_ref.1, f32[1]{0:T(128)S(6)} %copy.8.log_scale_ref, f32[1]{0:T(128)S(6)} %copy.9.bias_ref), custom_call_target="tpu_custom_call" | custom-call | tf_op jit(solution)/shard_map/pallas_call | solution.py:344
  75.3 1.4 %shard_map.78 = (bf16[384,1152]{1,0:T(8,128)(2,1)}, bf16[1152,640]{1,0:T(8,128)(2,1)}) custom-call(bf16[384,1152]{1,0:T(8,128)(2,1)S(1)} %get-tuple-element.4.cgrad_ref, bf16[1152,640]{1,0:T(8,128)(2,1)S(1)} %get-tuple-element.5.pgrad_ref), custom_call_target="tpu_custom_call" | custom-call | tf_op jit(solution)/shard_map/pallas_call | solution.py:396

commit v6 on v5

--- a/solution.py
+++ b/solution.py
@@ -27,8 +27,8 @@
 TILE = 16
 
 ORDERS = (("x", "y", "z"), ("y", "x", "z"), ("z", "x", "y"))
-PART = (256, 160, 160)
-FIRST = (0, 256, 416)
+PART = (224, 176, 176)
+FIRST = (0, 224, 400)
 PARTS = len(ORDERS)
 READY = (1, 2, 0)
 PIECES = 3
@@ -77,12 +77,16 @@
     own_core, own_x, relay, pool,
     out_core, in_core, own_term, s1_out, s1_in, s2_out, s2_in, s3_in, gather2, gather1, other1,
     load_sem, hop_send, hop_recv, swap_send, swap_recv, core_send, core_recv,
-    stage_send, stage_recv, last_send, last_recv, round_sem,
+    stage_send, stage_recv, last_send, last_recv, round_sem, second_sem,
 ):
     me = lax.axis_index("dp")
     core = place(me, "core")
     sibling = shifted(me, "core", 1)
 
+    barrier = pltpu.get_barrier_semaphore()
+    greeted = [*WAYS, ("x", 1), ("x", -1), ("core", 1)]
+    for axis, by in greeted:
+        pl.semaphore_signal(barrier, inc=1, device_id=(shifted(me, axis, by),), device_id_type=MESH)
     loads = [
         pltpu.make_async_copy(video_ref, video, load_sem.at[0]),
         pltpu.make_async_copy(captions_ref, captions, load_sem.at[1]),
@@ -91,13 +95,10 @@
     ]
     for load in loads:
         load.start()
-
-    barrier = pltpu.get_barrier_semaphore()
-    greeted = [(axis, way * by) for by in sorted({1, NEAR, REST}) for axis, way in WAYS]
-    greeted += [("x", 2), ("x", 1), ("x", -1), ("core", 1)]
-    for axis, by in greeted:
-        pl.semaphore_signal(barrier, inc=1, device_id=(shifted(me, axis, by),), device_id_type=MESH)
     pl.semaphore_wait(barrier, len(greeted))
+    first_round = [*WAYS, ("x", 1), ("x", -1)]
+    for axis, by in first_round:
+        pl.semaphore_signal(round_sem, inc=1, device_id=(shifted(me, axis, by),), device_id_type=MESH)
     loads[0].wait()
 
     hops = []
@@ -113,8 +114,6 @@
             )
             first.start()
             hops.append((first, second))
-    swap_x = remote(video, own_x, swap_send.at[0], swap_recv.at[0], shifted(me, "x", 2))
-    swap_x.start()
     swap_core = remote(video, own_core, swap_send.at[1], swap_recv.at[1], sibling)
     swap_core.start()
 
@@ -123,9 +122,11 @@
             first.wait_recv()
             second.start()
 
-    neighbours = [("y", 1), ("y", -1), ("z", 1), ("z", -1)]
-    for axis, by in neighbours:
-        pl.semaphore_signal(round_sem, inc=1, device_id=(shifted(me, axis, by),), device_id_type=MESH)
+    pl.semaphore_wait(round_sem, len(first_round))
+    for axis, way in WAYS:
+        pl.semaphore_signal(second_sem, inc=1, device_id=(shifted(me, axis, 2 * way),), device_id_type=MESH)
+    swap_x = remote(video, own_x, swap_send.at[0], swap_recv.at[0], shifted(me, "x", 2))
+    swap_x.start()
 
     scale = jnp.exp(jnp.full((1, 1), log_scale_ref[0], F32))
     shift = bias_ref[0]
@@ -152,6 +153,7 @@
             weight = sign / (1.0 + jnp.exp(-sign * logits))
         return jnp.dot(weight.astype(BF16), zv, preferred_element_type=F32)
 
+    pl.semaphore_wait(second_sem, len(WAYS))
     pass_on(0)
     row = lax.broadcasted_iota(jnp.int32, (ROWS, ROWS), 0)
     column = lax.broadcasted_iota(jnp.int32, (ROWS, ROWS), 1)
@@ -160,7 +162,6 @@
     for q in range(1, CHUNKS):
         pass_on(q)
     flipped[...] = captions[...].T
-    pl.semaphore_wait(round_sem, len(neighbours))
     swap_core.wait_recv()
     dz[...] += pairing(own_core[...])
     swap_x.wait_recv()
@@ -388,6 +389,7 @@
             dma((PARTS, 8)),
             dma((PARTS, 8)),
             pltpu.SemaphoreType.REGULAR,
+            pltpu.SemaphoreType.REGULAR,
         ],
         compiler_params=pltpu.CompilerParams(
             collective_id=0, has_side_effects=True, vmem_limit_bytes=40 << 20

time: 76.9 us -> 75.9 us (0.987)
  Pallas kernels: 74.8 us -> 73.9 us
    pallas_call x1, Pallas kernels: 73.3 us -> 72.4 us  [local(): pl.pallas_call(kernel, out_shape=(jax.ShapeDtypeStruct((ROWS, D), BF16),...]
where the time goes in v6:
time: 75.9 us; the launch traced here: 75.8 us
  Pallas kernels  73.9 us (97%)
  between operations  1.93 us (3%)
    pallas_call x1, Pallas kernels, local(): pl.pallas_call(kernel, out_shape=(jax.ShapeDtypeStruct((ROWS, D), BF16),...  72.4 us

profile of v6, /device:TPU:1, one launch (start us, length us, event | category | flops | bytes accessed | tf_op | source)
XLA Modules:
  0.0 75.8 jit_solution(11123791786758532660)
XLA Ops:
  1.9 72.4 %shard_map.77 = (bf16[384,1152]{1,0:T(8,128)(2,1)S(1)}, bf16[1152,640]{1,0:T(8,128)(2,1)S(1)}) custom-call(bf16[384,640]{1,0:T(8,128)(2,1)} %video_ref.1, bf16[384,1152]{1,0:T(8,128)(2,1)} %captions_ref.1, bf16[1152,640]{1,0:T(8,128)(2,1)} %projection_ref.1, s32[384]{0:T(512)} %labels_ref.1, f32[1]{0:T(128)S(6)} %copy.8.log_scale_ref, f32[1]{0:T(128)S(6)} %copy.9.bias_ref), custom_call_target="tpu_custom_call" | custom-call | tf_op jit(solution)/shard_map/pallas_call | solution.py:345
  74.4 1.4 %shard_map.78 = (bf16[384,1152]{1,0:T(8,128)(2,1)}, bf16[1152,640]{1,0:T(8,128)(2,1)}) custom-call(bf16[384,1152]{1,0:T(8,128)(2,1)S(1)} %get-tuple-element.4.cgrad_ref, bf16[1152,640]{1,0:T(8,128)(2,1)S(1)} %get-tuple-element.5.pgrad_ref), custom_call_target="tpu_custom_call" | custom-call | tf_op jit(solution)/shard_map/pallas_call | solution.py:398

commit v7 on v6

--- a/solution.py
+++ b/solution.py
@@ -18,7 +18,7 @@
 E = 640
 D = 1152
 HALF = D // 2
-CHUNKS = 3
+CHUNKS = 2
 CHUNK = ROWS // (2 * CHUNKS)
 NEAR, REST = 1, 3
 WAYS = (("y", 1), ("y", -1), ("z", 1), ("z", -1))

time: 75.9 us -> 75.6 us (level)
  no operation moved by 1% of the time
where the time goes in v7:
time: 75.6 us; the launch traced here: 75.4 us
  Pallas kernels  73.5 us (97%)
  between operations  1.93 us (3%)
    pallas_call x1, Pallas kernels, local(): pl.pallas_call(kernel, out_shape=(jax.ShapeDtypeStruct((ROWS, D), BF16),...  72 us

profile of v7, /device:TPU:1, one launch (start us, length us, event | category | flops | bytes accessed | tf_op | source)
XLA Modules:
  0.0 75.4 jit_solution(4314027093231124965)
XLA Ops:
  1.9 72.0 %shard_map.77 = (bf16[384,1152]{1,0:T(8,128)(2,1)S(1)}, bf16[1152,640]{1,0:T(8,128)(2,1)S(1)}) custom-call(bf16[384,640]{1,0:T(8,128)(2,1)} %video_ref.1, bf16[384,1152]{1,0:T(8,128)(2,1)} %captions_ref.1, bf16[1152,640]{1,0:T(8,128)(2,1)} %projection_ref.1, s32[384]{0:T(512)} %labels_ref.1, f32[1]{0:T(128)S(6)} %copy.8.log_scale_ref, f32[1]{0:T(128)S(6)} %copy.9.bias_ref), custom_call_target="tpu_custom_call" | custom-call | tf_op jit(solution)/shard_map/pallas_call | solution.py:345
  74.0 1.4 %shard_map.78 = (bf16[384,1152]{1,0:T(8,128)(2,1)}, bf16[1152,640]{1,0:T(8,128)(2,1)}) custom-call(bf16[384,1152]{1,0:T(8,128)(2,1)S(1)} %get-tuple-element.4.cgrad_ref, bf16[1152,640]{1,0:T(8,128)(2,1)S(1)} %get-tuple-element.5.pgrad_ref), custom_call_target="tpu_custom_call" | custom-call | tf_op jit(solution)/shard_map/pallas_call | solution.py:398
